TPU v7x, 128 devices: a whole 4x4x4 slice. The times are simulated.
128 devices in a mesh: lat: 16 (over y, z_lo, core), lon: 8 (over x, z_hi).
Axes of the slice: x: 4, y: 4, z: 4 (z_hi: 2, z_lo: 2; z = z_hi * 2 + z_lo), core: 2. Of those that a mesh axis runs over, the one named last changes fastest.
Arguments:
- fields: bfloat16 [128, 720, 6400], P(None, 'lon', 'lat'), may hold values from -6 to 6
- surf_weight: bfloat16 [4, 100, 512], replicated, may hold values from -0.625 to 0.625
- atmos_weight: bfloat16 [5, 100, 512], replicated, may hold values from -0.625 to 0.625
- level_bias_table: float32 [12, 512], replicated, may hold values from -6 to 6
- latents: bfloat16 [3, 512], replicated, may hold values from -6 to 6
- query_matrix: bfloat16 [512, 512], replicated, as said below
- key_weight: bfloat16 [512, 512], replicated, may hold values from -0.25 to 0.25
- value_weight: bfloat16 [512, 512], replicated, may hold values from -0.25 to 0.25
- out_weight: bfloat16 [512, 512], replicated, may hold values from -0.25 to 0.25
Outputs:
- encoded: bfloat16 [128, 720, 4, 512], P('lat', 'lon')
Inputs may be any that keep to these rules, and one draw needn't show every extreme that they name: `query_matrix`: entries of either sign, independent.
All inputs are finite; a program needn't handle non-finite values.
Results may differ from a plain program's by a relative error of at most 0.012.
The roundings to bfloat16 on the way count: a program that leaves them out, or rounds other values in their place, can miss the bound.
Values may be sent and summed in bfloat16 or wider, within the bound.
A program may use at most 192 MiB of HBM per device.

v0:
```python
import math

import jax
import jax.numpy as jnp
from jax import lax
from jax.sharding import PartitionSpec as P

C = 512
HEADS = 16
HEAD_CHANNELS = 32
PATCH = 10
NSURF = 4
NATM = 5
LATENT = 3
LEV = 12
F = 64


def encode(
    block,
    surf_weight,
    atmos_weight,
    level_bias_table,
    latents,
    query_matrix,
    key_weight,
    value_weight,
    out_weight,
):
    tok_rows = block.shape[0]
    tok_cols = block.shape[1]
    count = tok_rows * tok_cols
    patch_tokens = block.reshape(count, F, PATCH * PATCH)
    surface = jnp.dot(
        patch_tokens[:, :NSURF].reshape(count, NSURF * PATCH * PATCH),
        surf_weight.reshape(NSURF * PATCH * PATCH, C),
        preferred_element_type=jnp.float32,
    )
    levels = jnp.zeros((count, LEV, C), jnp.float32) + level_bias_table
    for var in range(NATM):
        start = NSURF + var * LEV
        levels = levels + jnp.einsum(
            "nlk,kc->nlc",
            patch_tokens[:, start : start + LEV],
            atmos_weight[var],
            preferred_element_type=jnp.float32,
        )
    centre = jnp.mean(levels, axis=-1, keepdims=True)
    spread = jnp.mean((levels - centre) ** 2, axis=-1, keepdims=True)
    normed = ((levels - centre) / jnp.sqrt(spread + 1e-05)).astype(jnp.bfloat16)
    key_vector = jnp.einsum(
        "nlc,cd->nld", normed, key_weight, preferred_element_type=jnp.float32
    ).astype(jnp.bfloat16)
    val_vec = jnp.einsum(
        "nlc,cd->nld", normed, value_weight, preferred_element_type=jnp.float32
    ).astype(jnp.bfloat16)
    key_vector = key_vector.reshape(count, LEV, HEADS, HEAD_CHANNELS)
    val_vec = val_vec.reshape(count, LEV, HEADS, HEAD_CHANNELS)
    query_rows = jnp.dot(latents, query_matrix, preferred_element_type=jnp.float32).astype(
        jnp.bfloat16
    )
    query_rows = query_rows.reshape(LATENT, HEADS, HEAD_CHANNELS)
    attention_logits = jnp.einsum(
        "qix,nlix->iqln", query_rows, key_vector, preferred_element_type=jnp.float32
    ) / math.sqrt(HEAD_CHANNELS)
    attention_logits = attention_logits - jnp.max(attention_logits, axis=2, keepdims=True)
    expo = jnp.exp(attention_logits)
    weights = (expo / jnp.sum(expo, axis=2, keepdims=True)).astype(jnp.bfloat16)
    mixture = jnp.einsum(
        "hmln,nlhd->nmhd", weights, val_vec, preferred_element_type=jnp.float32
    ).astype(jnp.bfloat16)
    mixture = mixture.reshape(count, LATENT, C)
    aggregated = latents.astype(jnp.float32) + jnp.einsum(
        "nmc,cd->nmd", mixture, out_weight, preferred_element_type=jnp.float32
    )
    joined = jnp.concatenate([surface[:, None, :], aggregated], axis=1).astype(jnp.bfloat16)
    return joined.reshape(tok_rows, tok_cols, LATENT + 1, C)


def shards(
    fields,
    surf_weight,
    atmos_weight,
    level_bias_table,
    latents,
    query_matrix,
    key_weight,
    value_weight,
    out_weight,
):
    blocked = lax.all_to_all(fields, "lat", split_axis=0, concat_axis=2, tiled=True)
    encoded = encode(
        blocked,
        surf_weight,
        atmos_weight,
        level_bias_table,
        latents,
        query_matrix,
        key_weight,
        value_weight,
        out_weight,
    )
    return encoded


def solution(mesh):
    in_specs = (P(None, "lon", "lat"), P(), P(), P(), P(), P(), P(), P(), P())
    out_specs = P("lat", "lon", None, None)
    return jax.shard_map(shards, mesh=mesh, in_specs=in_specs, out_specs=out_specs, check_vma=False)
```

profile of v0, /device:TPU:1, one launch (start us, length us, event | category | flops | bytes accessed | tf_op | source)
XLA Modules:
  0.0 541.5 jit_solution(14848432845787778883)
XLA Ops:
  0.0 0.0 copy-start
  0.0 16.9 %copy.30 = bf16[128,90,400]{2,1,0:T(8,128)(2,1)} copy(bf16[128,90,400]{0,2,1:T(8,128)(2,1)} %param.9) | data formatting | bytes 18432000 | tf_op args[0]
  16.9 0.0 copy-start.8
  16.9 0.0 copy-start.6
  16.9 7.5 %all-to-all-start = ((bf16[128,90,400]{2,1,0:T(8,128)(2,1)}), bf16[128,90,400]{2,1,0:T(8,128)(2,1)}, u32[]{:S(2)}, u32[]{:S(2)}) async-start(bf16[128,90,400]{2,1,0:T(8,128)(2,1)} %copy.30), calls=%async_computation | async-start | bytes 25165824 | tf_op jit(solution)/shard_map/all_to_all | solution.py:91
  24.4 0.0 copy-done.8
  24.4 0.6 convert_element_type.26
  25.0 0.0 copy-done.6
  25.0 0.2 convolution_convert_fusion.2
  25.2 0.1 reshape.43
  25.3 199.3 %all-to-all-done = bf16[128,90,400]{2,1,0:T(8,128)(2,1)} async-done(((bf16[128,90,400]{2,1,0:T(8,128)(2,1)}), bf16[128,90,400]{2,1,0:T(8,128)(2,1)}, u32[]{:S(2)}, u32[]{:S(2)}) %all-to-all-start) | async-done | bytes 9216032 | tf_op jit(solution)/shard_map/all_to_all | solution.py:91
  224.6 22.1 %copy.32 = bf16[8,90,16,400]{1,0,3,2:T(8,128)(2,1)} copy(bf16[8,90,16,400]{3,1,0,2:T(8,128)(2,1)} %bitcast.2) | data formatting | bytes 18432000 | tf_op jit(solution)/shard_map/all_to_all | solution.py:91
  246.6 0.0 copy-start.5
  246.6 21.2 %reshape.40 = bf16[720,64,100]{0,2,1:T(8,128)(2,1)} reshape(bf16[8,90,16,400]{1,0,3,2:T(8,128)(2,1)} %copy.32) | data formatting | bytes 18432000 | tf_op jit(solution)/shard_map/reshape | solution.py:33
  267.8 0.0 copy-done.5
  267.8 0.0 copy-start.3
  267.8 10.4 %fusion.11 = f32[720,12,512]{2,0,1:T(8,128)} fusion(bf16[720,64,100]{0,2,1:T(8,128)(2,1)} %reshape.40, bf16[5,100,512]{2,1,0:T(8,128)(2,1)S(1)} %copy-done.5), kind=kOutput, calls=%fused_computation.24 | convolution fusion | flops 884736000 | bytes 27017216 | tf_op jit(solution)/shard_map/nlk,kc->nlc/dot_general | solution.py:42
  278.2 0.0 copy-done.3
  278.2 8.6 %fusion.13 = f32[720,12,512]{2,0,1:T(8,128)} fusion(bf16[720,64,100]{0,2,1:T(8,128)(2,1)S(1)} %copy-done.3, bf16[5,100,512]{2,1,0:T(8,128)(2,1)S(1)} %copy-done.5), kind=kOutput, calls=%fused_computation.26 | convolution fusion | flops 884736000 | bytes 28024832 | tf_op jit(solution)/shard_map/nlk,kc->nlc/dot_general | solution.py:42
  286.8 8.7 %fusion.15 = f32[720,12,512]{2,0,1:T(8,128)} fusion(bf16[720,64,100]{0,2,1:T(8,128)(2,1)S(1)} %copy-done.3, bf16[5,100,512]{2,1,0:T(8,128)(2,1)S(1)} %copy-done.5), kind=kOutput, calls=%fused_computation.28 | convolution fusion | flops 884736000 | bytes 28024832 | tf_op jit(solution)/shard_map/nlk,kc->nlc/dot_general | solution.py:42
  295.5 0.0 copy-start.7
  295.5 8.7 %fusion.9 = f32[720,12,512]{2,0,1:T(8,128)} fusion(bf16[720,64,100]{0,2,1:T(8,128)(2,1)S(1)} %copy-done.3, bf16[5,100,512]{2,1,0:T(8,128)(2,1)S(1)} %copy-done.5), kind=kOutput, calls=%fused_computation.22 | convolution fusion | flops 884736000 | bytes 28024832 | tf_op jit(solution)/shard_map/nlk,kc->nlc/dot_general | solution.py:42
  304.2 0.0 copy-done.7
  304.2 30.7 %fusion.23 = (f32[720,12]{0,1:T(8,128)S(1)}, f32[720,12,512]{2,0,1:T(8,128)}) fusion(bf16[720,64,100]{0,2,1:T(8,128)(2,1)} %reshape.40, bf16[5,100,512]{2,1,0:T(8,128)(2,1)S(1)} %copy-done.5, f32[720,12,512]{2,0,1:T(8,128)} %fusion.9, f32[720,12,512]{2,0,1:T(8,128)} %fusion.11, f32[720,12,512]{2,0,1:T(8,128)} %fusion.13, f32[720,12,512]{2,0,1:T(8,128)} %fusion.15, ...), kind=kOutput, calls=%fused_computation.38 | convolution fusion | flops 911269440 | bytes 97863424 | tf_op jit(solution)/shard_map/nlk,kc->nlc/dot_general | solution.py:42
  334.9 0.0 copy-start.2
  334.9 8.8 %multiply_reduce_fusion = f32[720,12]{0,1:T(8,128)S(1)} fusion(f32[720,12,512]{2,0,1:T(8,128)} %get-tuple-element.6, f32[720,12]{0,1:T(8,128)S(1)} %broadcast_multiply_fusion), kind=kLoop, calls=%fused_computation.1 | loop fusion | flops 13262400 | bytes 17763840 | tf_op jit(solution)/shard_map/reduce_sum | solution.py:49
  343.7 2.4 copy-done.2
  346.1 2.9 divide_convert_fusion
  349.1 0.0 copy-start.4
  349.1 3.4 copy-done.4
  352.4 0.0 copy-done
  352.4 7.1 %convolution_convert_fusion = bf16[720,12,512]{2,0,1:T(8,128)(2,1)} fusion(bf16[720,12,512]{2,0,1:T(8,128)(2,1)S(1)} %divide_convert_fusion, bf16[512,512]{1,0:T(8,128)(2,1)S(1)} %copy-done), kind=kOutput, calls=%fused_computation.6 | convolution fusion | flops 4534272000 | bytes 18219008 | tf_op jit(solution)/shard_map/nlc,cd->nld/dot_general | solution.py:51
  359.6 12.2 %copy.35 = bf16[720,12,512]{0,2,1:T(8,128)(2,1)} copy(bf16[720,12,512]{2,0,1:T(8,128)(2,1)} %convolution_convert_fusion) | data formatting | bytes 17694720 | tf_op jit(solution)/shard_map/convert_element_type | solution.py:53
  371.7 5.1 bitcast_reduce_fusion
  376.8 0.0 copy-start.10
  376.9 1.0 fusion.3
  377.9 1.0 divide_convert_fusion.1
  378.9 15.7 %copy.39 = bf16[16,3,12,720]{2,1,0,3:T(4,128)(2,1)} copy(bf16[16,3,12,720]{3,1,2,0:T(4,128)(2,1)S(1)} %divide_convert_fusion.1) | data formatting | bytes 1658880 | tf_op jit(solution)/shard_map/convert_element_type | solution.py:68
  394.6 0.0 copy-done.10
  394.6 10.5 %convolution_convert_fusion.1 = bf16[720,12,512]{2,0,1:T(8,128)(2,1)} fusion(bf16[720,12,512]{2,0,1:T(8,128)(2,1)} %copy-done.4, bf16[512,512]{1,0:T(8,128)(2,1)S(1)} %copy-done.10), kind=kOutput, calls=%fused_computation.7 | convolution fusion | flops 4534272000 | bytes 18219008 | tf_op jit(solution)/shard_map/nlc,cd->nld/dot_general | solution.py:54
  405.1 12.4 %copy.34 = bf16[720,12,512]{0,2,1:T(8,128)(2,1)} copy(bf16[720,12,512]{2,0,1:T(8,128)(2,1)} %convolution_convert_fusion.1) | data formatting | bytes 17694720 | tf_op jit(solution)/shard_map/convert_element_type | solution.py:56
  417.6 66.9 %copy.38 = bf16[720,12,16,32]{3,1,2,0:T(8,128)(2,1)} copy(bf16[720,12,16,32]{0,3,2,1:T(8,128)(2,1)} %bitcast.70) | data formatting | bytes 17694720 | tf_op jit(solution)/shard_map/reshape | solution.py:58
  484.5 25.2 %convert_bitcast_fusion = bf16[720,3,16,32]{3,1,2,0:T(4,128)(2,1)} fusion(bf16[720,12,16,32]{3,1,2,0:T(8,128)(2,1)} %copy.38, bf16[16,3,12,720]{2,1,0,3:T(4,128)(2,1)} %copy.39), kind=kOutput, calls=%fused_computation.3 | convolution fusion | flops 27648000 | bytes 11888640 | tf_op jit(solution)/shard_map/hmln,nlhd->nmhd/dot_general | solution.py:69
  509.7 0.0 copy-start.9
  509.7 0.0 copy-start.11
  509.7 16.3 %copy.40 = bf16[720,3,16,32]{0,3,2,1:T(8,128)(2,1)S(1)} copy(bf16[720,3,16,32]{3,1,2,0:T(4,128)(2,1)} %convert_bitcast_fusion) | data formatting | bytes 4423680 | tf_op jit(solution)/shard_map/convert_element_type | solution.py:71
  526.0 0.0 copy-done.9
  526.0 0.0 copy-done.11
  526.0 0.0 copy-start.1
  526.0 2.7 add_convert_fusion
  528.8 2.6 concatenate.10
  531.4 2.7 bitcast_convert_fusion
  534.0 2.2 concatenate.9
  536.2 1.4 pad_maximum_fusion
  537.7 3.9 copy.42
  541.5 0.0 copy-done.1
  (2 shorter events, 0.0 us)
Async XLA Ops:
  0.0 352.4 %copy-start = (bf16[512,512]{1,0:T(8,128)(2,1)S(1)}, bf16[512,512]{1,0:T(8,128)(2,1)}, u32[]{:S(2)}) copy-start(bf16[512,512]{1,0:T(8,128)(2,1)} %param.15) | copy-start | bytes 1572868
  16.9 7.5 %copy-start.8 = (bf16[3,512]{1,0:T(4,128)(2,1)S(1)}, bf16[3,512]{1,0:T(4,128)(2,1)}, u32[]{:S(2)}) copy-start(bf16[3,512]{1,0:T(4,128)(2,1)} %param.13) | copy-start | bytes 9220
  16.9 8.1 %copy-start.6 = (bf16[512,512]{1,0:T(8,128)(2,1)S(1)}, bf16[512,512]{1,0:T(8,128)(2,1)}, u32[]{:S(2)}) copy-start(bf16[512,512]{1,0:T(8,128)(2,1)} %param.14) | copy-start | bytes 1572868
  16.9 207.7 %all-to-all-start = ((bf16[128,90,400]{2,1,0:T(8,128)(2,1)}), bf16[128,90,400]{2,1,0:T(8,128)(2,1)}, u32[]{:S(2)}, u32[]{:S(2)}) async-start(bf16[128,90,400]{2,1,0:T(8,128)(2,1)} %copy.30), calls=%async_computation | async-start | bytes 25165824 | tf_op jit(solution)/shard_map/all_to_all | solution.py:91
  246.6 21.2 %copy-start.5 = (bf16[5,100,512]{2,1,0:T(8,128)(2,1)S(1)}, bf16[5,100,512]{2,1,0:T(8,128)(2,1)}, u32[]{:S(2)}) copy-start(bf16[5,100,512]{2,1,0:T(8,128)(2,1)} %param.11) | copy-start | bytes 1536004
  267.8 10.4 %copy-start.3 = (bf16[720,64,100]{0,2,1:T(8,128)(2,1)S(1)}, bf16[720,64,100]{0,2,1:T(8,128)(2,1)}, u32[]{:S(2)}) copy-start(bf16[720,64,100]{0,2,1:T(8,128)(2,1)} %reshape.40) | copy-start | bytes 27648004
  295.5 8.7 %copy-start.7 = (f32[12,512]{1,0:T(8,128)S(1)}, f32[12,512]{1,0:T(8,128)}, u32[]{:S(2)}) copy-start(f32[12,512]{1,0:T(8,128)} %param.12) | copy-start | bytes 73732
  334.9 11.2 %copy-start.2 = (f32[720,12,512]{2,0,1:T(8,128)S(1)}, f32[720,12,512]{2,0,1:T(8,128)}, u32[]{:S(2)}) copy-start(f32[720,12,512]{2,0,1:T(8,128)} %get-tuple-element.6) | copy-start | bytes 53084164
  349.1 3.4 copy-start.4
  376.8 17.8 %copy-start.10 = (bf16[512,512]{1,0:T(8,128)(2,1)S(1)}, bf16[512,512]{1,0:T(8,128)(2,1)}, u32[]{:S(2)}) copy-start(bf16[512,512]{1,0:T(8,128)(2,1)} %param.16) | copy-start | bytes 1572868
  509.7 16.3 %copy-start.9 = (f32[3,512]{1,0:T(4,128)S(1)}, f32[3,512]{1,0:T(4,128)}, u32[]{:S(2)}) copy-start(f32[3,512]{1,0:T(4,128)} %convert_element_type.26) | copy-start | bytes 18436
  509.7 16.3 %copy-start.11 = (bf16[512,512]{1,0:T(8,128)(2,1)S(1)}, bf16[512,512]{1,0:T(8,128)(2,1)}, u32[]{:S(2)}) copy-start(bf16[512,512]{1,0:T(8,128)(2,1)} %param.17) | copy-start | bytes 1572868
  526.0 15.5 %copy-start.1 = (bf16[512,512]{1,0:T(8,128)(2,1)S(1)}, bf16[512,512]{1,0:T(8,128)(2,1)}, u32[]{:S(2)}) copy-start(bf16[512,512]{1,0:T(8,128)(2,1)} %param.15) | copy-start | bytes 1572868
where the time goes:
time: 544 us; the launch traced here: 542 us
  waiting for transfers between devices  199 us (37%)
  local copies, waits for them, and re-layouts  198 us (36%)
  matrix products  121 us (22%)
  other arithmetic  15.8 us (3%)
  starting transfers between devices  7.47 us (1%)
    all_to_all x1, waiting for transfers between devices, shards(): lax.all_to_all(fields, 'lat', split_axis=0, concat_axis=2, tiled=True)  199 us
    dot_general x5, matrix products, encode(): jnp.einsum('nlk,kc->nlc', patch_tokens[:, start:start + LEV], atmos_weigh...  67.1 us
    reshape x1, local copies, waits for them, and re-layouts, encode(): val_vec = val_vec.reshape(count, LEV, HEADS, HEAD_CHANNELS)  66.9 us
    dot_general x1, matrix products, encode(): jnp.einsum('hmln,nlhd->nmhd', weights, val_vec, preferred_element_type=jn...  25.2 us
    unnamed x25, local copies, waits for them, and re-layouts  22.7 us
    all_to_all x1, local copies, waits for them, and re-layouts, shards(): lax.all_to_all(fields, 'lat', split_axis=0, concat_axis=2, tiled=True)  22.1 us
    reshape x1, local copies, waits for them, and re-layouts, encode(): patch_tokens = block.reshape(count, F, PATCH * PATCH)  21.2 us
    convert_element_type x1, local copies, waits for them, and re-layouts, encode(): mixture = jnp.einsum('hmln,nlhd->nmhd', weights, val_vec, preferred_eleme...  16.3 us
  transfers between devices with their start and end apart: 1, of which 1 were waited for; matrix products, arithmetic and copies ran while one was open for 0% of the time, Pallas kernels for 0%

commit v1 on v0

v1 whole, which is shorter than its diff:
```python
import functools
import math

import jax
import jax.numpy as jnp
from jax import lax
from jax.experimental import pallas as pl
from jax.experimental.pallas import tpu as pltpu
from jax.sharding import PartitionSpec as P

C = 512
HEADS = 16
HEAD_CHANNELS = 32
K = 100
NSURF = 4
NATM = 5
LATENT = 3
LEV = 12
NDEV = 16
FPD = 4
ROWS = 400
A = 8
COLS = 90
LANES = 128
BLK = 16
FULL = 5
REST = 10
REST_ROWS = 256
KT = 25
PAIRS = LEV // 2
QROWS = LATENT * HEADS

MESH = pl.DeviceIdType.MESH
BF16 = jnp.bfloat16
F32 = jnp.float32


def far_first():
    offsets = [(dy, dz, dc) for dy in range(4) for dz in range(2) for dc in range(2)][1:]
    return sorted(offsets, key=lambda o: -(min(o[0], 4 - o[0]) + o[1]))


OFFSETS = far_first()


def peer_of(me, offset):
    dy, dz, dc = offset
    y, z, c = me // 4, (me // 2) % 2, me % 2
    return ((y + dy) % 4) * 4 + ((z + dz) % 2) * 2 + (c + dc) % 2


def block_transpose(parts):
    lane = lax.broadcasted_iota(jnp.int32, parts[0].shape, 1)
    turned = [x if j == 0 else pltpu.roll(x, 8 * j, 1) for j, x in enumerate(parts)]
    held = [turned[-e % BLK] for e in range(BLK)]
    for s in (1, 2, 4, 8):
        mask = (lane & (8 * s)) != 0
        held = [jnp.where(mask, held[(e - s) % BLK], held[e]) for e in range(BLK)]
    return held


def kernel(
    fields_ref, surf_ref, atmos_ref, bias_ref, lat_ref, qm_ref, kw_ref, vw_ref, ow_ref,
    out_ref,
    inb, send, recv, unpacked, xs, wat, wvu, wsurf, biasb, vals, scores, mix, slots, outb,
    surf_v, atmos_v, bias_v, lat_v, qm_v, kw_v, vw_v, ow_v,
    in_sem, w_sem, send_sem, recv_sem, self_sem, out_sem,
):
    me = lax.axis_index("lat")

    loads = []
    for c in range(FULL + 1):
        n = BLK if c < FULL else REST
        loads.append(pltpu.make_async_copy(
            fields_ref.at[pl.ds(BLK * c, n)], inb.at[pl.ds(BLK * c, n)], in_sem.at[c]))
    loads[0].start()
    barrier = pltpu.get_barrier_semaphore()
    for o in OFFSETS:
        pl.semaphore_signal(barrier, inc=1, device_id={"lat": peer_of(me, o)}, device_id_type=MESH)
    for load in loads[1:]:
        load.start()
    weight_loads = []
    for i, (src, dst) in enumerate((
        (qm_ref, qm_v), (lat_ref, lat_v), (kw_ref, kw_v), (vw_ref, vw_v), (atmos_ref, atmos_v),
        (surf_ref, surf_v), (bias_ref, bias_v), (ow_ref, ow_v),
    )):
        weight_loads.append(pltpu.make_async_copy(src, dst, w_sem.at[i]))
        weight_loads[-1].start()

    def shuffle_full(c):
        def tile(t, carry):
            rows = pl.ds(pl.multiple_of(16 * t, 16), 16)
            parts = [inb[BLK * c + j, rows, :] for j in range(BLK)]
            for e, y in enumerate(block_transpose(parts)):
                send[c, e, rows, :] = y
            return carry
        lax.fori_loop(0, KT, tile, 0)

    def shuffle_rest():
        def group(g, carry):
            parts = []
            for j in range(BLK):
                n = lax.rem(BLK * g + j, KT * REST)
                t = n // REST
                parts.append(inb[BLK * FULL + n - t * REST, pl.ds(pl.multiple_of(16 * t, 16), 16), :])
            rows = pl.ds(pl.multiple_of(16 * g, 16), 16)
            for e, y in enumerate(block_transpose(parts)):
                send[FULL, e, rows, :] = y if e == 0 else pltpu.roll(y, LANES - 8 * e, 1)
            return carry
        lax.fori_loop(0, BLK, group, 0)

    def own(c):
        rows = pl.ds(0, ROWS if c < FULL else REST_ROWS)
        return pltpu.make_async_copy(send.at[c, me, rows], recv.at[c, me, rows], self_sem.at[c])

    def ship(c):
        rows = pl.ds(0, ROWS if c < FULL else REST_ROWS)
        for o in OFFSETS:
            d = peer_of(me, o)
            pltpu.make_async_remote_copy(
                src_ref=send.at[c, d, rows], dst_ref=recv.at[c, me, rows],
                send_sem=send_sem.at[c], recv_sem=recv_sem.at[c],
                device_id={"lat": d}, device_id_type=MESH,
            ).start()
        own(c).start()

    for c in range(FULL + 1):
        loads[c].wait()
        if c < FULL:
            shuffle_full(c)
        else:
            shuffle_rest()
        if c == 0:
            pl.semaphore_wait(barrier, NDEV - 1)
        ship(c)

    for load in weight_loads:
        load.wait()
    queries = jnp.dot(lat_v[...], qm_v[...], preferred_element_type=F32).astype(BF16).astype(F32)
    channel_head = lax.broadcasted_iota(jnp.int32, (HEADS, C), 1) // HEAD_CHANNELS
    own_head = channel_head == lax.broadcasted_iota(jnp.int32, (HEADS, C), 0)
    spread = jnp.concatenate(
        [jnp.where(own_head, jnp.broadcast_to(queries[m : m + 1], (HEADS, C)), 0.0) for m in range(LATENT)],
        axis=0,
    ).astype(BF16)
    score_w = lax.dot_general(
        spread, kw_v[...], (((1,), (1,)), ((), ())), preferred_element_type=F32
    ) * (1.0 / math.sqrt(HEAD_CHANNELS))
    high = score_w.astype(BF16)
    wvu[pl.ds(0, C), :] = vw_v[...].astype(F32).T.astype(BF16)
    wvu[pl.ds(C, QROWS), :] = high
    wvu[pl.ds(C + QROWS, QROWS), :] = (score_w - high.astype(F32)).astype(BF16)
    stacked = jnp.concatenate(
        [atmos_v[v].astype(F32) for v in range(NATM)] + [jnp.zeros((C - NATM * K, C), F32)], axis=0
    )
    wat[...] = stacked.T.astype(BF16)
    wsurf[...] = jnp.concatenate([surf_v[f].astype(F32) for f in range(NSURF)], axis=0).astype(BF16)

    def spread_bias(l, carry):
        row = bias_v[pl.ds(l, 1), :]
        biasb[l] = jnp.broadcast_to(row, (LANES, C)).T
        return carry
    lax.fori_loop(0, LEV, spread_bias, 0)
    xs[:, pl.ds(C - 16, 16), :] = jnp.zeros((PAIRS, 16, 2 * LANES), BF16)

    def unpack(s, carry):
        lane = lax.broadcasted_iota(jnp.int32, (16, LANES), 1)
        for t in range(KT):
            g, off = divmod(8 * REST * t, LANES)
            x = recv[FULL, s, 16 * g : 16 * g + 16, :]
            if off:
                x = pltpu.roll(x, LANES - off, 1)
            if off + 8 * REST > LANES:
                y = pltpu.roll(recv[FULL, s, 16 * g + 16 : 16 * g + 32, :], LANES - off, 1)
                x = jnp.where(lane < LANES - off, x, y)
            unpacked[s, 16 * t : 16 * t + 16, :] = x
        return carry

    def out_copy(c, slot):
        n = BLK if c < FULL else REST
        return pltpu.make_async_copy(
            outb.at[slot, :, pl.ds(0, n)], out_ref.at[:, pl.ds(BLK * c, n)], out_sem.at[slot])

    def process(block, turn, slot):
        for s in range(1, NDEV):
            v, g = divmod(s - 1, 3)
            for j in range(FPD):
                l = 4 * g + j
                xs[l // 2, pl.ds(K * v, K), pl.ds((l % 2) * LANES, LANES)] = block[s, pl.ds(K * j, K), :]

        def pair(p, carry):
            levels = jnp.dot(wat[...], xs[p], preferred_element_type=F32)
            levels = levels + jnp.concatenate([biasb[2 * p], biasb[2 * p + 1]], axis=1)
            centred = levels - jnp.sum(levels, axis=0, keepdims=True) * (1.0 / C)
            var = jnp.sum(centred * centred, axis=0, keepdims=True) * (1.0 / C)
            normed = (centred * lax.rsqrt(var + 1e-5)).astype(BF16)
            got = jnp.dot(wvu[...], normed, preferred_element_type=F32)
            for i in range(2):
                half = got[:, i * LANES : (i + 1) * LANES]
                vals[2 * p + i] = half[:C].astype(BF16)
                scores[2 * p + i] = half[C : C + QROWS] + half[C + QROWS :]
            return carry
        lax.fori_loop(0, PAIRS, pair, 0)

        top = scores[0]
        for l in range(1, LEV):
            top = jnp.maximum(top, scores[l])
        total = jnp.zeros((QROWS, LANES), F32)
        for l in range(LEV):
            e = jnp.exp(scores[l] - top)
            scores[l] = e
            total = total + e
        for l in range(LEV):
            scores[l] = (scores[l] / total).astype(BF16).astype(F32)

        def head(h, carry):
            rows = pl.ds(pl.multiple_of(HEAD_CHANNELS * h, HEAD_CHANNELS), HEAD_CHANNELS)
            sums = [jnp.zeros((HEAD_CHANNELS, LANES), F32) for _ in range(LATENT)]
            for l in range(LEV):
                val = vals[l, rows, :].astype(F32)
                for m in range(LATENT):
                    sums[m] = sums[m] + scores[l, pl.ds(m * HEADS + h, 1), :] * val
            for m in range(LATENT):
                mix[m, rows, :] = sums[m].astype(BF16)
            return carry
        lax.fori_loop(0, HEADS, head, 0)

        surf = lax.dot_general(block[0], wsurf[...], (((0,), (0,)), ((), ())), preferred_element_type=F32)
        slots[:, 0, :] = surf
        for m in range(LATENT):
            agg = lax.dot_general(mix[m], ow_v[...], (((0,), (0,)), ((), ())), preferred_element_type=F32)
            slots[:, m + 1, :] = agg + lat_v[pl.ds(m, 1), :].astype(F32)

        def place(j, carry):
            start = pl.multiple_of(A * lax.rem(j + turn, BLK), A)
            for a in range(A):
                outb[slot, a, j] = slots[start + a].astype(BF16)
            return carry
        lax.fori_loop(0, BLK, place, 0)

    def wait_recv(c):
        rows = pl.ds(0, ROWS if c < FULL else REST_ROWS)
        whole = recv.at[c, pl.ds(0, NDEV - 1), rows]
        pltpu.make_async_copy(whole, whole, recv_sem.at[c]).wait()
        own(c).wait()

    for c in range(FULL + 1):
        slot = c % 2
        wait_recv(c)
        if c >= 2:
            out_copy(c - 2, slot).wait()
        if c < FULL:
            process(recv.at[c], me, slot)
        else:
            lax.fori_loop(0, NDEV, unpack, 0)
            process(unpacked, 0, slot)
        out_copy(c, slot).start()
    out_copy(FULL - 1, (FULL - 1) % 2).wait()
    out_copy(FULL, FULL % 2).wait()
    for c in range(FULL + 1):
        rows = pl.ds(0, ROWS if c < FULL else REST_ROWS)
        whole = send.at[c, pl.ds(0, NDEV - 1), rows]
        pltpu.make_async_copy(whole, whole, send_sem.at[c]).wait()


def shards(fields, surf_weight, atmos_weight, level_bias_table, latents, query_matrix, key_weight, value_weight, out_weight):
    by_token = jnp.transpose(fields, (1, 2, 0))
    any_spec = pl.BlockSpec(memory_space=pl.ANY)
    dma = pltpu.SemaphoreType.DMA
    return pl.pallas_call(
        kernel,
        out_shape=jax.ShapeDtypeStruct((A, COLS, LATENT + 1, C), BF16),
        in_specs=[any_spec] * 9,
        out_specs=any_spec,
        scratch_shapes=[
            pltpu.VMEM((COLS, ROWS, LANES), BF16),
            pltpu.VMEM((FULL + 1, NDEV, ROWS, LANES), BF16),
            pltpu.VMEM((FULL + 1, NDEV, ROWS, LANES), BF16),
            pltpu.VMEM((NDEV, ROWS, LANES), BF16),
            pltpu.VMEM((PAIRS, C, 2 * LANES), BF16),
            pltpu.VMEM((C, C), BF16),
            pltpu.VMEM((C + 2 * QROWS, C), BF16),
            pltpu.VMEM((NSURF * K, C), BF16),
            pltpu.VMEM((LEV, C, LANES), F32),
            pltpu.VMEM((LEV, C, LANES), BF16),
            pltpu.VMEM((LEV, QROWS, LANES), F32),
            pltpu.VMEM((LATENT, C, LANES), BF16),
            pltpu.VMEM((LANES, LATENT + 1, C), F32),
            pltpu.VMEM((2, A, BLK, LATENT + 1, C), BF16),
            pltpu.VMEM(surf_weight.shape, BF16),
            pltpu.VMEM(atmos_weight.shape, BF16),
            pltpu.VMEM(level_bias_table.shape, F32),
            pltpu.VMEM(latents.shape, BF16),
            pltpu.VMEM(query_matrix.shape, BF16),
            pltpu.VMEM(key_weight.shape, BF16),
            pltpu.VMEM(value_weight.shape, BF16),
            pltpu.VMEM(out_weight.shape, BF16),
            dma((FULL + 1,)),
            dma((8,)),
            dma((FULL + 1,)),
            dma((FULL + 1,)),
            dma((FULL + 1,)),
            dma((2,)),
        ],
        compiler_params=pltpu.CompilerParams(
            collective_id=0, has_side_effects=True, vmem_limit_bytes=60 * 2**20
        ),
        name="exchange_and_encode",
    )(by_token, surf_weight, atmos_weight, level_bias_table, latents, query_matrix, key_weight, value_weight, out_weight)


def solution(mesh):
    in_specs = (P(None, "lon", "lat"), P(), P(), P(), P(), P(), P(), P(), P())
    out_specs = P("lat", "lon", None, None)
    return jax.shard_map(shards, mesh=mesh, in_specs=in_specs, out_specs=out_specs, check_vma=False)
```

time: 544 us -> 127 us (0.23)
  waiting for transfers between devices: 199 us -> 0 us
  local copies, waits for them, and re-layouts: 198 us -> 6.27 us
  matrix products: 121 us -> 0 us
  Pallas kernels: 0 us -> 119 us
  other arithmetic: 15.8 us -> 0 us
  starting transfers between devices: 7.47 us -> 0 us
    all_to_all x1 -> x0, waiting for transfers between devices: 199 us -> none  [shards(): lax.all_to_all(fields, 'lat', split_axis=0, concat_axis=2, tiled=True)]
    dot_general x12 -> x0, matrix products: 121 us -> none  [the longest x5 67.1 us: encode(): jnp.einsum('nlk,kc->nlc', patch_tokens[:, start:start + LEV], atmos_weigh...]
    pallas_call x0 -> x1, Pallas kernels: none -> 119 us  [shards(): pl.pallas_call(kernel, out_shape=jax.ShapeDtypeStruct((A, COLS, LATENT +...]
    reshape x3 -> x0, local copies, waits for them, and re-layouts: 88.2 us -> none  [the longest x1 66.9 us: encode(): val_vec = val_vec.reshape(count, LEV, HEADS, HEAD_CHANNELS)]
    convert_element_type x4 -> x0, local copies, waits for them, and re-layouts: 56.6 us -> none  [the longest x1 16.3 us: encode(): mixture = jnp.einsum('hmln,nlhd->nmhd', weights, val_vec, preferred_eleme...]
    all_to_all x1 -> x0, local copies, waits for them, and re-layouts: 22.1 us -> none  [shards(): lax.all_to_all(fields, 'lat', split_axis=0, concat_axis=2, tiled=True)]
    unnamed x25 -> x2, local copies, waits for them, and re-layouts: 22.7 us -> 6.27 us
    reduce_sum x2 -> x0, other arithmetic: 9.81 us -> none  [the longest x1 8.78 us: encode(): spread = jnp.mean((levels - centre) ** 2, axis=-1, keepdims=True)]
  transfers between devices with their start and end apart: 1 -> 0, of which waited for: 1 -> 0; matrix products, arithmetic and copies ran while one was open for 0% -> 0% of each run, Pallas kernels for 0% -> 0%
where the time goes in v1:
time: 127 us; the launch traced here: 125 us
  Pallas kernels  119 us (94%)
  local copies, waits for them, and re-layouts  6.27 us (5%)
    pallas_call x1, Pallas kernels, shards(): pl.pallas_call(kernel, out_shape=jax.ShapeDtypeStruct((A, COLS, LATENT +...  119 us
    unnamed x2, local copies, waits for them, and re-layouts  6.27 us

profile of v1, /device:TPU:1, one launch (start us, length us, event | category | flops | bytes accessed | tf_op | source)
XLA Modules:
  0.0 125.2 jit_solution(5505899506191419283)
XLA Ops:
  0.0 1.8 %copy.10.surf_ref = bf16[4,100,512]{2,1,0:T(8,128)(2,1)} copy(bf16[4,100,512]{2,0,1:T(4,128)(2,1)} %param.10) | data formatting | bytes 819200 | tf_op args[1]
  1.8 118.9 %exchange_and_encode.1 = bf16[8,90,4,512]{3,2,1,0:T(4,128)(2,1)} custom-call(bf16[90,400,128]{2,1,0:T(8,128)(2,1)} %bitcast.1, bf16[4,100,512]{2,1,0:T(8,128)(2,1)} %copy.10.surf_ref, bf16[5,100,512]{2,1,0:T(8,128)(2,1)} %atmos_ref.1, f32[12,512]{1,0:T(8,128)} %bias_ref.1, bf16[3,512]{1,0:T(4,128)(2,1)} %lat_ref.1, bf16[512,512]{1,0:T(8,128)(2,1)} %qm_ref.1, ...), custom_call_target="tpu_custom_call" | custom-call | tf_op jit(solution)/shard_map/exchange_and_encode/pallas_call | solution.py:270
  120.7 4.4 %copy.12 = bf16[8,90,4,512]{3,2,1,0:T(4,128)(2,1)} copy(bf16[8,90,4,512]{3,2,1,0:T(4,128)(2,1)} %exchange_and_encode.1) | data formatting | bytes 5898240

commit v2 on v1

v2 whole, which is shorter than its diff:
```python
import functools
import math

import jax
import jax.numpy as jnp
from jax import lax
from jax.experimental import pallas as pl
from jax.experimental.pallas import tpu as pltpu
from jax.sharding import PartitionSpec as P

C = 512
HEADS = 16
HEAD_CHANNELS = 32
K = 100
NSURF = 4
NATM = 5
LATENT = 3
LEV = 12
NDEV = 16
FPD = 4
ROWS = 400
A = 8
COLS = 90
LANES = 128
BLK = 16
FULL = 5
REST = 10
REST_ROWS = 256
KT = 25
QROWS = LATENT * HEADS
LAST = FULL - 1
PIECES = ((0, 208), (208, 304), (304, 400))
EARLY = 5 * BLK

MESH = pl.DeviceIdType.MESH
BF16 = jnp.bfloat16
F32 = jnp.float32


def far_first():
    offsets = [(dy, dz, dc) for dy in range(4) for dz in range(2) for dc in range(2)][1:]
    return sorted(offsets, key=lambda o: -(min(o[0], 4 - o[0]) + o[1]))


OFFSETS = far_first()


def peer_of(me, offset):
    dy, dz, dc = offset
    y, z, c = me // 4, (me // 2) % 2, me % 2
    return ((y + dy) % 4) * 4 + ((z + dz) % 2) * 2 + (c + dc) % 2


def block_transpose(parts):
    lane = lax.broadcasted_iota(jnp.int32, parts[0].shape, 1)
    turned = [x if j == 0 else pltpu.roll(x, 8 * j, 1) for j, x in enumerate(parts)]
    held = [turned[-e % BLK] for e in range(BLK)]
    for s in (1, 2, 4, 8):
        mask = (lane & (8 * s)) != 0
        held = [jnp.where(mask, held[(e - s) % BLK], held[e]) for e in range(BLK)]
    return held


def project(block, mix, wsurf, ow, lat, slots):
    contract = (((0,), (0,)), ((), ()))
    slots[:, 0, :] = lax.dot_general(block[...], wsurf[...], contract, preferred_element_type=F32)
    for m in range(LATENT):
        agg = lax.dot_general(mix[m], ow[...], contract, preferred_element_type=F32)
        slots[:, m + 1, :] = agg + lat[pl.ds(m, 1), :].astype(F32)


def kernel(
    fields_ref, surf_ref, atmos_ref, bias_ref, lat_ref, qm_ref, kw_ref, vw_ref, ow_ref,
    staged, mix, last_surf, wsurf, ow_v, lat_v,
    inb, send, recv, xs, wat, wvu, biasb, vals, scores, slots,
    surf_v, atmos_v, bias_v, qm_v, kw_v, vw_v,
    in_sem, w_sem, send_sem, recv_sem, piece_sem, self_sem,
):
    me = lax.axis_index("lat")
    rest_raw, rest_done = FULL, FULL + 1

    def load(c, n=BLK):
        here = pl.ds(BLK * c, n)
        return pltpu.make_async_copy(fields_ref.at[here], inb.at[here], in_sem.at[c])

    load(0).start()
    barrier = pltpu.get_barrier_semaphore()
    for o in OFFSETS:
        pl.semaphore_signal(barrier, inc=1, device_id={"lat": peer_of(me, o)}, device_id_type=MESH)
    for c in range(1, FULL):
        load(c).start()
    load(FULL, REST).start()
    weight_loads = []
    for i, (src, dst) in enumerate((
        (qm_ref, qm_v), (lat_ref, lat_v), (kw_ref, kw_v), (vw_ref, vw_v), (atmos_ref, atmos_v),
        (surf_ref, surf_v), (bias_ref, bias_v), (ow_ref, ow_v),
    )):
        weight_loads.append(pltpu.make_async_copy(src, dst, w_sem.at[i]))
        weight_loads[-1].start()

    def unturn(e, y):
        return y if e == 0 else pltpu.roll(y, LANES - 8 * e, 1)

    def shuffle_full(c, straight=False):
        def tile(t, carry):
            rows = pl.ds(pl.multiple_of(16 * t, 16), 16)
            parts = [inb[BLK * c + j, rows, :] for j in range(BLK)]
            for e, y in enumerate(block_transpose(parts)):
                send[c, e, rows, :] = unturn(e, y) if straight else y
            return carry
        lax.fori_loop(0, KT, tile, 0, unroll=5)

    def rest_group(q, g, count):
        parts = []
        for j in range(BLK):
            t, b = divmod(BLK * g + j, REST) if j < count else (0, j - count)
            rows = pl.ds(pl.multiple_of(128 * q + 16 * t, 16), 16)
            parts.append(inb[BLK * FULL + b, rows, :])
        rows = pl.ds(pl.multiple_of(80 * q + 16 * g, 16), 16)
        for e, y in enumerate(block_transpose(parts)):
            send[FULL, e, rows, :] = unturn(e, y)

    def shuffle_rest():
        def five(q, carry):
            for g in range(5):
                rest_group(q, g, BLK)
            return carry
        lax.fori_loop(0, 3, five, 0)
        rest_group(3, 0, REST)

    def own(c, start, stop, sem):
        rows = pl.ds(start, stop - start)
        return pltpu.make_async_copy(send.at[c, me, rows], recv.at[c, me, rows], sem)

    def ship(c, start, stop, sem, own_sem):
        rows = pl.ds(start, stop - start)
        for o in OFFSETS:
            d = peer_of(me, o)
            pltpu.make_async_remote_copy(
                src_ref=send.at[c, d, rows], dst_ref=recv.at[c, me, rows],
                send_sem=send_sem.at[c], recv_sem=sem,
                device_id={"lat": d}, device_id_type=MESH,
            ).start()
        own(c, start, stop, own_sem).start()

    def ship_whole(c, rows):
        ship(c, 0, rows, recv_sem.at[c], self_sem.at[c])

    load(0).wait()
    shuffle_full(0)
    pl.semaphore_wait(barrier, NDEV - 1)
    ship_whole(0, ROWS)

    def send_next(c, carry):
        load(c).wait()
        shuffle_full(c)
        ship_whole(c, ROWS)
        return carry
    lax.fori_loop(1, LAST, send_next, 0)
    load(FULL, REST).wait()
    shuffle_rest()
    ship_whole(FULL, REST_ROWS)
    load(LAST).wait()
    shuffle_full(LAST, straight=True)
    for i, (start, stop) in enumerate(PIECES):
        ship(LAST, start, stop, piece_sem.at[i], self_sem.at[FULL + 1 + i])

    for w in weight_loads:
        w.wait()
    queries = jnp.dot(lat_v[...], qm_v[...], preferred_element_type=F32).astype(BF16).astype(F32)
    channel_head = lax.broadcasted_iota(jnp.int32, (HEADS, C), 1) // HEAD_CHANNELS
    own_head = channel_head == lax.broadcasted_iota(jnp.int32, (HEADS, C), 0)
    spread = jnp.concatenate(
        [jnp.where(own_head, jnp.broadcast_to(queries[m : m + 1], (HEADS, C)), 0.0) for m in range(LATENT)],
        axis=0,
    ).astype(BF16)
    score_w = lax.dot_general(
        spread, kw_v[...], (((1,), (1,)), ((), ())), preferred_element_type=F32
    ) * (1.0 / math.sqrt(HEAD_CHANNELS))
    high = score_w.astype(BF16)
    wvu[pl.ds(0, C), :] = vw_v[...].astype(F32).T.astype(BF16)
    wvu[pl.ds(C, QROWS), :] = high
    wvu[pl.ds(C + QROWS, QROWS), :] = (score_w - high.astype(F32)).astype(BF16)
    stacked = jnp.concatenate(
        [atmos_v[v].astype(F32) for v in range(NATM)] + [jnp.zeros((C - NATM * K, C), F32)], axis=0
    )
    wat[...] = stacked.T.astype(BF16)
    wsurf[...] = jnp.concatenate([surf_v[:, f, :].astype(F32) for f in range(NSURF)], axis=0).astype(BF16)

    for n in range(LEV):
        l = 4 * (n % 3) + n // 3
        biasb[n] = jnp.broadcast_to(bias_v[pl.ds(l, 1), :], (LANES, C)).T
    xs[pl.ds(C - 16, 16), :] = jnp.zeros((16, LEV * LANES), BF16)

    def unpack(s, carry):
        lane = lax.broadcasted_iota(jnp.int32, (16, LANES), 1)
        for t in range(KT):
            g, off = divmod(8 * REST * t, LANES)
            x = recv[rest_raw, s, 16 * g : 16 * g + 16, :]
            if off:
                x = pltpu.roll(x, LANES - off, 1)
            if off + 8 * REST > LANES:
                y = pltpu.roll(recv[rest_raw, s, 16 * g + 16 : 16 * g + 32, :], LANES - off, 1)
                x = jnp.where(lane < LANES - off, x, y)
            recv[rest_done, s, 16 * t : 16 * t + 16, :] = x
        return carry

    def gather(place, j):
        for s in range(1, NDEV):
            v, g = divmod(s - 1, 3)
            xs[pl.ds(K * v, K), pl.ds((3 * j + g) * LANES, LANES)] = recv[place, s, pl.ds(K * j, K), :]

    def embed(first, count):
        cols = pl.ds(first * LANES, count * LANES)
        levels = jnp.dot(wat[...], xs[:, cols], preferred_element_type=F32)
        levels = levels + jnp.concatenate([biasb[first + i] for i in range(count)], axis=1)
        centred = levels - jnp.sum(levels, axis=0, keepdims=True) * (1.0 / C)
        var = jnp.sum(centred * centred, axis=0, keepdims=True) * (1.0 / C)
        xs[:, cols] = (centred * lax.rsqrt(var + 1e-5)).astype(BF16)

    def attend(first, count):
        got = jnp.dot(wvu[...], xs[:, pl.ds(first * LANES, count * LANES)], preferred_element_type=F32)
        for i in range(count):
            part = got[:, i * LANES : (i + 1) * LANES]
            vals[first + i] = part[:C].astype(BF16)
            scores[first + i] = part[C : C + QROWS] + part[C + QROWS :]

    def softmax():
        top = scores[0]
        for l in range(1, LEV):
            top = jnp.maximum(top, scores[l])
        total = jnp.zeros((QROWS, LANES), F32)
        for l in range(LEV):
            e = jnp.exp(scores[l] - top)
            scores[l] = e
            total = total + e
        for l in range(LEV):
            scores[l] = (scores[l] / total).astype(BF16).astype(F32)

    def mixture():
        def head(h, carry):
            rows = pl.ds(pl.multiple_of(HEAD_CHANNELS * h, HEAD_CHANNELS), HEAD_CHANNELS)
            sums = [jnp.zeros((HEAD_CHANNELS, LANES), F32) for _ in range(LATENT)]
            for l in range(LEV):
                val = vals[l, rows, :].astype(F32)
                for m in range(LATENT):
                    sums[m] = sums[m] + scores[l, pl.ds(m * HEADS + h, 1), :] * val
            for m in range(LATENT):
                mix[m, rows, :] = sums[m].astype(BF16)
            return carry
        lax.fori_loop(0, HEADS, head, 0)

    def lay_out(t, turn):
        def move(j, carry):
            start = pl.multiple_of(A * lax.rem(j + turn, BLK), A)
            for a in range(A):
                staged[a, BLK * t + j] = slots[start + a].astype(BF16)
            return carry
        lax.fori_loop(0, BLK, move, 0, unroll=2)

    def arrived(c, start, stop, sem, own_sem):
        whole = recv.at[c, pl.ds(0, NDEV - 1), pl.ds(start, stop - start)]
        pltpu.make_async_copy(whole, whole, sem).wait()
        own(c, start, stop, own_sem).wait()

    def process(t, carry):
        is_rest = t // LAST
        place = t + is_rest * (rest_done - LAST)

        @pl.when(t < LAST)
        def _():
            arrived(t, 0, ROWS, recv_sem.at[t], self_sem.at[t])

        @pl.when(t == LAST)
        def _():
            arrived(FULL, 0, REST_ROWS, recv_sem.at[FULL], self_sem.at[FULL])
            lax.fori_loop(0, NDEV, unpack, 0, unroll=2)

        for j in range(FPD):
            gather(place, j)
        for p in range(LEV // 2):
            embed(2 * p, 2)
        for p in range(LEV // 2):
            attend(2 * p, 2)
        softmax()
        mixture()
        project(recv.at[place, 0], mix, wsurf, ow_v, lat_v, slots)
        lay_out(t, me * (1 - is_rest))
        return carry
    lax.fori_loop(0, FULL, process, 0)

    done = 0
    for i, (start, stop) in enumerate(PIECES):
        arrived(LAST, start, stop, piece_sem.at[i], self_sem.at[FULL + 1 + i])
        while done < FPD and K * (done + 1) <= stop:
            gather(LAST, done)
            done += 1
        if i == 0:
            groups = ((0, 2), (2, 2), (4, 2))
        else:
            groups = ((3 * (done - 1), 3),)
        for group in groups:
            embed(*group)
        for group in groups:
            attend(*group)
        rows = pl.ds(start, stop - start)
        last_surf[rows, :] = recv[LAST, 0, rows, :]
    softmax()
    mixture()

    for c in range(FULL + 1):
        whole = send.at[c, pl.ds(0, NDEV - 1), pl.ds(0, ROWS if c < FULL else REST_ROWS)]
        pltpu.make_async_copy(whole, whole, send_sem.at[c]).wait()


def finish(staged, mix, last_surf, wsurf, ow, lat, out_ref, slots, outb, sem):
    ahead = BLK * LAST
    writes = [
        pltpu.make_async_copy(staged.at[:, pl.ds(0, ahead)], out_ref.at[:, pl.ds(0, ahead)], sem.at[0]),
        pltpu.make_async_copy(staged.at[:, pl.ds(ahead, REST)], out_ref.at[:, pl.ds(BLK * FULL, REST)], sem.at[1]),
    ]
    for write in writes:
        write.start()
    project(last_surf, mix, wsurf, ow, lat, slots)

    def move(j, carry):
        start = pl.multiple_of(A * j, A)
        for a in range(A):
            outb[a, j] = slots[start + a].astype(BF16)
        return carry
    lax.fori_loop(0, BLK, move, 0, unroll=2)
    writes.append(pltpu.make_async_copy(outb, out_ref.at[:, pl.ds(ahead, BLK)], sem.at[2]))
    writes[-1].start()
    for write in writes:
        write.wait()


def shards(fields, surf_weight, atmos_weight, level_bias_table, latents, query_matrix, key_weight, value_weight, out_weight):
    by_token = jnp.transpose(fields, (1, 2, 0))
    surf_cells = jnp.transpose(surf_weight, (1, 0, 2))
    operands = (
        by_token, surf_cells, atmos_weight, level_bias_table, latents,
        query_matrix, key_weight, value_weight, out_weight,
    )
    in_hbm = pl.BlockSpec(memory_space=pl.ANY)
    in_vmem = pl.BlockSpec(memory_space=pltpu.VMEM)
    dma = pltpu.SemaphoreType.DMA
    handed = pl.pallas_call(
        kernel,
        out_shape=[
            pltpu.VMEM((A, EARLY, LATENT + 1, C), BF16),
            pltpu.VMEM((LATENT, C, LANES), BF16),
            pltpu.VMEM((ROWS, LANES), BF16),
            pltpu.VMEM((NSURF * K, C), BF16),
            pltpu.VMEM((C, C), BF16),
            pltpu.VMEM((LATENT, C), BF16),
        ],
        in_specs=[in_hbm] * 9,
        out_specs=[in_vmem] * 6,
        scratch_shapes=[
            pltpu.VMEM((COLS, ROWS, LANES), BF16),
            pltpu.VMEM((FULL + 1, NDEV, ROWS, LANES), BF16),
            pltpu.VMEM((FULL + 2, NDEV, ROWS, LANES), BF16),
            pltpu.VMEM((C, LEV * LANES), BF16),
            pltpu.VMEM((C, C), BF16),
            pltpu.VMEM((C + 2 * QROWS, C), BF16),
            pltpu.VMEM((LEV, C, LANES), F32),
            pltpu.VMEM((LEV, C, LANES), BF16),
            pltpu.VMEM((LEV, QROWS, LANES), F32),
            pltpu.VMEM((LANES, LATENT + 1, C), F32),
            pltpu.VMEM(surf_cells.shape, BF16),
            pltpu.VMEM(atmos_weight.shape, BF16),
            pltpu.VMEM(level_bias_table.shape, F32),
            pltpu.VMEM(query_matrix.shape, BF16),
            pltpu.VMEM(key_weight.shape, BF16),
            pltpu.VMEM(value_weight.shape, BF16),
            dma((FULL + 1,)),
            dma((8,)),
            dma((FULL + 1,)),
            dma((FULL + 1,)),
            dma((len(PIECES),)),
            dma((FULL + 1 + len(PIECES),)),
        ],
        compiler_params=pltpu.CompilerParams(
            collective_id=0, has_side_effects=True, vmem_limit_bytes=48 * 2**20
        ),
        name="exchange_and_encode",
    )(*[pltpu.with_memory_space_constraint(x, pltpu.HBM) for x in operands])
    return pl.pallas_call(
        finish,
        out_shape=jax.ShapeDtypeStruct((A, COLS, LATENT + 1, C), BF16),
        in_specs=[in_vmem] * 6,
        out_specs=in_hbm,
        scratch_shapes=[
            pltpu.VMEM((LANES, LATENT + 1, C), F32),
            pltpu.VMEM((A, BLK, LATENT + 1, C), BF16),
            dma((3,)),
        ],
        compiler_params=pltpu.CompilerParams(vmem_limit_bytes=8 * 2**20),
        name="finish",
    )(*[pltpu.with_memory_space_constraint(x, pltpu.VMEM) for x in handed])


def solution(mesh):
    in_specs = (P(None, "lon", "lat"), P(), P(), P(), P(), P(), P(), P(), P())
    out_specs = P("lat", "lon", None, None)
    return jax.shard_map(shards, mesh=mesh, in_specs=in_specs, out_specs=out_specs, check_vma=False)
```

time: 127 us -> 113 us (0.89); the launches traced: 125 us -> 112 us
  Pallas kernels: 119 us -> 112 us
  local copies, waits for them, and re-layouts: 6.27 us -> 0 us
    pallas_call x1 -> x2, Pallas kernels: 119 us -> 112 us  [the longest x1 111 us: shards(): pl.pallas_call(kernel, out_shape=[pltpu.VMEM((A, EARLY, LATENT + 1, C), B...]
    unnamed x2 -> x0, local copies, waits for them, and re-layouts: 6.27 us -> none
where the time goes in v2:
time: 113 us; the launch traced here: 112 us
  Pallas kernels  112 us (99%)
    pallas_call x1, Pallas kernels, shards(): pl.pallas_call(kernel, out_shape=[pltpu.VMEM((A, EARLY, LATENT + 1, C), B...  111 us

profile of v2, /device:TPU:1, one launch (start us, length us, event | category | flops | bytes accessed | tf_op | source)
XLA Modules:
  0.0 112.5 jit_solution(13084970645740226104)
XLA Ops:
  0.0 110.8 %exchange_and_encode.1 = (bf16[8,80,4,512]{3,2,1,0:T(4,128)(2,1)S(1)}, bf16[3,512,128]{2,1,0:T(8,128)(2,1)S(1)}, bf16[400,128]{1,0:T(8,128)(2,1)S(1)}, bf16[400,...) custom-call(bf16[90,400,128]{2,1,0:T(8,128)(2,1)} %bitcast.2, ...), custom_call_target="tpu_custom_call" | custom-call | tf_op jit(solution)/shard_map/exchange_and_encode/pallas_call | solution.py:348
  110.8 1.6 %finish.1 = bf16[8,90,4,512]{3,2,1,0:T(4,128)(2,1)} custom-call(bf16[8,80,4,512]{3,2,1,0:T(4,128)(2,1)S(1)} %get-tuple-element.11.staged, bf16[3,512,128]{2,1,0:T(8,128)(2,1)S(1)} %get-tuple-element.12.mix, bf16[400,128]{1,0:T(8,128)(2,1)S(1)} %get-tuple-element.13.last_surf, bf16[400,512]{1,0:T(8,128)(2,1)S(1)} %get-tuple-element.14.wsurf, ...), custom_call_target="tpu_custom_call" | custom-call | tf_op jit(solution)/shard_map/finish/pallas_call | solution.py:389

commit v3 on v2

--- a/solution.py
+++ b/solution.py
@@ -29,6 +29,7 @@
 KT = 25
 QROWS = LATENT * HEADS
 LAST = FULL - 1
+OPENING = 80
 PIECES = ((0, 208), (208, 304), (304, 400))
 EARLY = 5 * BLK
 
@@ -61,6 +62,19 @@
     return held
 
 
+def mixture(terms, shares, out):
+    for h in range(HEADS):
+        rows = pl.ds(HEAD_CHANNELS * h, HEAD_CHANNELS)
+        sums = [None] * LATENT
+        for i, values in terms:
+            held = [values(m)[rows, :] for m in range(LATENT)] if callable(values) else [values[rows, :]] * LATENT
+            for m in range(LATENT):
+                term = shares[i, pl.ds(m * HEADS + h, 1), :] * held[m]
+                sums[m] = term if sums[m] is None else sums[m] + term
+        for m in range(LATENT):
+            out[m, rows, :] = sums[m].astype(out.dtype)
+
+
 def project(block, mix, wsurf, ow, lat, slots):
     contract = (((0,), (0,)), ((), ()))
     slots[:, 0, :] = lax.dot_general(block[...], wsurf[...], contract, preferred_element_type=F32)
@@ -72,21 +86,23 @@
 def kernel(
     fields_ref, surf_ref, atmos_ref, bias_ref, lat_ref, qm_ref, kw_ref, vw_ref, ow_ref,
     staged, mix, last_surf, wsurf, ow_v, lat_v,
-    inb, send, recv, xs, wat, wvu, biasb, vals, scores, slots,
+    inb, send, recv, xs, wat, wuv, biasb, vals, scores, part, slots,
     surf_v, atmos_v, bias_v, qm_v, kw_v, vw_v,
     in_sem, w_sem, send_sem, recv_sem, piece_sem, self_sem,
 ):
     me = lax.axis_index("lat")
     rest_raw, rest_done = FULL, FULL + 1
 
-    def load(c, n=BLK):
-        here = pl.ds(BLK * c, n)
-        return pltpu.make_async_copy(fields_ref.at[here], inb.at[here], in_sem.at[c])
-
-    load(0).start()
+    def load(c, n=BLK, start=0, stop=ROWS, sem=None):
+        here, rows = pl.ds(BLK * c, n), pl.ds(start, stop - start)
+        return pltpu.make_async_copy(
+            fields_ref.at[here, rows], inb.at[here, rows], in_sem.at[c if sem is None else sem])
+
+    load(0, stop=OPENING).start()
     barrier = pltpu.get_barrier_semaphore()
     for o in OFFSETS:
         pl.semaphore_signal(barrier, inc=1, device_id={"lat": peer_of(me, o)}, device_id_type=MESH)
+    load(0, start=OPENING, sem=FULL + 1).start()
     for c in range(1, FULL):
         load(c).start()
     load(FULL, REST).start()
@@ -101,14 +117,14 @@
     def unturn(e, y):
         return y if e == 0 else pltpu.roll(y, LANES - 8 * e, 1)
 
-    def shuffle_full(c, straight=False):
+    def shuffle_full(c, straight=False, start=0, stop=ROWS):
         def tile(t, carry):
             rows = pl.ds(pl.multiple_of(16 * t, 16), 16)
             parts = [inb[BLK * c + j, rows, :] for j in range(BLK)]
             for e, y in enumerate(block_transpose(parts)):
                 send[c, e, rows, :] = unturn(e, y) if straight else y
             return carry
-        lax.fori_loop(0, KT, tile, 0, unroll=5)
+        lax.fori_loop(start // 16, stop // 16, tile, 0, unroll=5)
 
     def rest_group(q, g, count):
         parts = []
@@ -146,10 +162,13 @@
     def ship_whole(c, rows):
         ship(c, 0, rows, recv_sem.at[c], self_sem.at[c])
 
-    load(0).wait()
-    shuffle_full(0)
+    load(0, stop=OPENING).wait()
+    shuffle_full(0, stop=OPENING)
     pl.semaphore_wait(barrier, NDEV - 1)
-    ship_whole(0, ROWS)
+    ship(0, 0, OPENING, recv_sem.at[0], self_sem.at[0])
+    load(0, start=OPENING, sem=FULL + 1).wait()
+    shuffle_full(0, start=OPENING)
+    ship(0, OPENING, ROWS, recv_sem.at[0], self_sem.at[0])
 
     def send_next(c, carry):
         load(c).wait()
@@ -178,9 +197,9 @@
         spread, kw_v[...], (((1,), (1,)), ((), ())), preferred_element_type=F32
     ) * (1.0 / math.sqrt(HEAD_CHANNELS))
     high = score_w.astype(BF16)
-    wvu[pl.ds(0, C), :] = vw_v[...].astype(F32).T.astype(BF16)
-    wvu[pl.ds(C, QROWS), :] = high
-    wvu[pl.ds(C + QROWS, QROWS), :] = (score_w - high.astype(F32)).astype(BF16)
+    wuv[pl.ds(0, QROWS), :] = high
+    wuv[pl.ds(QROWS, QROWS), :] = (score_w - high.astype(F32)).astype(BF16)
+    wuv[pl.ds(2 * QROWS, C), :] = vw_v[...].astype(F32).T.astype(BF16)
     stacked = jnp.concatenate(
         [atmos_v[v].astype(F32) for v in range(NATM)] + [jnp.zeros((C - NATM * K, C), F32)], axis=0
     )
@@ -219,11 +238,11 @@
         xs[:, cols] = (centred * lax.rsqrt(var + 1e-5)).astype(BF16)
 
     def attend(first, count):
-        got = jnp.dot(wvu[...], xs[:, pl.ds(first * LANES, count * LANES)], preferred_element_type=F32)
+        got = jnp.dot(wuv[...], xs[:, pl.ds(first * LANES, count * LANES)], preferred_element_type=F32)
         for i in range(count):
             part = got[:, i * LANES : (i + 1) * LANES]
-            vals[first + i] = part[:C].astype(BF16)
-            scores[first + i] = part[C : C + QROWS] + part[C + QROWS :]
+            scores[first + i] = part[:QROWS] + part[QROWS : 2 * QROWS]
+            vals[first + i] = part[2 * QROWS :].astype(BF16).astype(F32)
 
     def softmax():
         top = scores[0]
@@ -237,19 +256,6 @@
         for l in range(LEV):
             scores[l] = (scores[l] / total).astype(BF16).astype(F32)
 
-    def mixture():
-        def head(h, carry):
-            rows = pl.ds(pl.multiple_of(HEAD_CHANNELS * h, HEAD_CHANNELS), HEAD_CHANNELS)
-            sums = [jnp.zeros((HEAD_CHANNELS, LANES), F32) for _ in range(LATENT)]
-            for l in range(LEV):
-                val = vals[l, rows, :].astype(F32)
-                for m in range(LATENT):
-                    sums[m] = sums[m] + scores[l, pl.ds(m * HEADS + h, 1), :] * val
-            for m in range(LATENT):
-                mix[m, rows, :] = sums[m].astype(BF16)
-            return carry
-        lax.fori_loop(0, HEADS, head, 0)
-
     def lay_out(t, turn):
         def move(j, carry):
             start = pl.multiple_of(A * lax.rem(j + turn, BLK), A)
@@ -283,30 +289,55 @@
         for p in range(LEV // 2):
             attend(2 * p, 2)
         softmax()
-        mixture()
+        mixture([(l, vals.at[l]) for l in range(LEV)], scores, mix)
         project(recv.at[place, 0], mix, wsurf, ow_v, lat_v, slots)
         lay_out(t, me * (1 - is_rest))
         return carry
     lax.fori_loop(0, FULL, process, 0)
 
-    done = 0
-    for i, (start, stop) in enumerate(PIECES):
+    def piece(i):
+        start, stop = PIECES[i]
         arrived(LAST, start, stop, piece_sem.at[i], self_sem.at[FULL + 1 + i])
-        while done < FPD and K * (done + 1) <= stop:
-            gather(LAST, done)
-            done += 1
-        if i == 0:
-            groups = ((0, 2), (2, 2), (4, 2))
-        else:
-            groups = ((3 * (done - 1), 3),)
-        for group in groups:
-            embed(*group)
-        for group in groups:
-            attend(*group)
         rows = pl.ds(start, stop - start)
         last_surf[rows, :] = recv[LAST, 0, rows, :]
-    softmax()
-    mixture()
+
+    early = LEV - 3
+    piece(0)
+    for j in range(2):
+        gather(LAST, j)
+    for p in range(3):
+        embed(2 * p, 2)
+    for p in range(3):
+        attend(2 * p, 2)
+    piece(1)
+    gather(LAST, 2)
+    embed(6, 3)
+    attend(6, 3)
+    top = scores[0]
+    for l in range(1, early):
+        top = jnp.maximum(top, scores[l])
+    total = jnp.zeros((QROWS, LANES), F32)
+    for l in range(early):
+        e = jnp.exp(scores[l] - top)
+        scores[l] = e
+        total = total + e
+    mixture([(l, vals.at[l]) for l in range(early)], scores, part)
+    scores[0] = top
+    scores[1] = total
+
+    piece(2)
+    gather(LAST, 3)
+    embed(early, 3)
+    attend(early, 3)
+    last = [scores[l] for l in range(early, LEV)]
+    top = jnp.maximum(jnp.maximum(last[0], last[1]), jnp.maximum(last[2], scores[0]))
+    last = [jnp.exp(x - top) for x in last]
+    scale = jnp.exp(scores[0] - top)
+    share = 1.0 / (last[0] + last[1] + last[2] + scale * scores[1])
+    scores[0] = scale * share
+    for i, e in enumerate(last):
+        scores[early + i] = e * share
+    mixture([(0, lambda m: part.at[m])] + [(l, vals.at[l]) for l in range(early, LEV)], scores, mix)
 
     for c in range(FULL + 1):
         whole = send.at[c, pl.ds(0, NDEV - 1), pl.ds(0, ROWS if c < FULL else REST_ROWS)]
@@ -328,9 +359,12 @@
         for a in range(A):
             outb[a, j] = slots[start + a].astype(BF16)
         return carry
-    lax.fori_loop(0, BLK, move, 0, unroll=2)
-    writes.append(pltpu.make_async_copy(outb, out_ref.at[:, pl.ds(ahead, BLK)], sem.at[2]))
-    writes[-1].start()
+    half = BLK // 2
+    for i in range(2):
+        lax.fori_loop(half * i, half * (i + 1), move, 0, unroll=4)
+        writes.append(pltpu.make_async_copy(
+            outb.at[:, pl.ds(half * i, half)], out_ref.at[:, pl.ds(ahead + half * i, half)], sem.at[2 + i]))
+        writes[-1].start()
     for write in writes:
         write.wait()
 
@@ -365,8 +399,9 @@
             pltpu.VMEM((C, C), BF16),
             pltpu.VMEM((C + 2 * QROWS, C), BF16),
             pltpu.VMEM((LEV, C, LANES), F32),
-            pltpu.VMEM((LEV, C, LANES), BF16),
+            pltpu.VMEM((LEV, C, LANES), F32),
             pltpu.VMEM((LEV, QROWS, LANES), F32),
+            pltpu.VMEM((LATENT, C, LANES), F32),
             pltpu.VMEM((LANES, LATENT + 1, C), F32),
             pltpu.VMEM(surf_cells.shape, BF16),
             pltpu.VMEM(atmos_weight.shape, BF16),
@@ -374,7 +409,7 @@
             pltpu.VMEM(query_matrix.shape, BF16),
             pltpu.VMEM(key_weight.shape, BF16),
             pltpu.VMEM(value_weight.shape, BF16),
-            dma((FULL + 1,)),
+            dma((FULL + 2,)),
             dma((8,)),
             dma((FULL + 1,)),
             dma((FULL + 1,)),
@@ -394,7 +429,7 @@
         scratch_shapes=[
             pltpu.VMEM((LANES, LATENT + 1, C), F32),
             pltpu.VMEM((A, BLK, LATENT + 1, C), BF16),
-            dma((3,)),
+            dma((4,)),
         ],
         compiler_params=pltpu.CompilerParams(vmem_limit_bytes=8 * 2**20),
         name="finish",

time: 113 us -> 112 us (level)
  no operation moved by 1% of the time
where the time goes in v3:
time: 112 us
  Pallas kernels  112 us (100%)
    pallas_call x1, Pallas kernels, shards(): pl.pallas_call(kernel, out_shape=[pltpu.VMEM((A, EARLY, LATENT + 1, C), B...  110 us

profile of v3, /device:TPU:1, one launch (start us, length us, event | category | flops | bytes accessed | tf_op | source)
XLA Modules:
  0.0 111.8 jit_solution(9282530901121463796)
XLA Ops:
  0.0 110.1 %exchange_and_encode.1 = (bf16[8,80,4,512]{3,2,1,0:T(4,128)(2,1)S(1)}, bf16[3,512,128]{2,1,0:T(8,128)(2,1)S(1)}, bf16[400,128]{1,0:T(8,128)(2,1)S(1)}, bf16[400,...) custom-call(bf16[90,400,128]{2,1,0:T(8,128)(2,1)} %bitcast.2, ...), custom_call_target="tpu_custom_call" | custom-call | tf_op jit(solution)/shard_map/exchange_and_encode/pallas_call | solution.py:382
  110.1 1.6 %finish.1 = bf16[8,90,4,512]{3,2,1,0:T(4,128)(2,1)} custom-call(bf16[8,80,4,512]{3,2,1,0:T(4,128)(2,1)S(1)} %get-tuple-element.11.staged, bf16[3,512,128]{2,1,0:T(8,128)(2,1)S(1)} %get-tuple-element.12.mix, bf16[400,128]{1,0:T(8,128)(2,1)S(1)} %get-tuple-element.13.last_surf, bf16[400,512]{1,0:T(8,128)(2,1)S(1)} %get-tuple-element.14.wsurf, ...), custom_call_target="tpu_custom_call" | custom-call | tf_op jit(solution)/shard_map/finish/pallas_call | solution.py:424

commit v4 on v3

--- a/solution.py
+++ b/solution.py
@@ -30,7 +30,8 @@
 QROWS = LATENT * HEADS
 LAST = FULL - 1
 OPENING = 80
-PIECES = ((0, 208), (208, 304), (304, 400))
+PIECES = ((0, 208), (208, 400))
+EARLY_LEVELS = 6
 EARLY = 5 * BLK
 
 MESH = pl.DeviceIdType.MESH
@@ -44,6 +45,8 @@
 
 
 OFFSETS = far_first()
+FAR = [o for o in OFFSETS if min(o[0], 4 - o[0]) + o[1] >= 2]
+NEAR = [o for o in OFFSETS if o not in FAR]
 
 
 def peer_of(me, offset):
@@ -148,16 +151,17 @@
         rows = pl.ds(start, stop - start)
         return pltpu.make_async_copy(send.at[c, me, rows], recv.at[c, me, rows], sem)
 
-    def ship(c, start, stop, sem, own_sem):
+    def ship(c, start, stop, sem, own_sem, offsets=OFFSETS):
         rows = pl.ds(start, stop - start)
-        for o in OFFSETS:
+        for o in offsets:
             d = peer_of(me, o)
             pltpu.make_async_remote_copy(
                 src_ref=send.at[c, d, rows], dst_ref=recv.at[c, me, rows],
                 send_sem=send_sem.at[c], recv_sem=sem,
                 device_id={"lat": d}, device_id_type=MESH,
             ).start()
-        own(c, start, stop, own_sem).start()
+        if own_sem is not None:
+            own(c, start, stop, own_sem).start()
 
     def ship_whole(c, rows):
         ship(c, 0, rows, recv_sem.at[c], self_sem.at[c])
@@ -181,8 +185,11 @@
     ship_whole(FULL, REST_ROWS)
     load(LAST).wait()
     shuffle_full(LAST, straight=True)
+    for o in FAR:
+        for i, (start, stop) in enumerate(PIECES):
+            ship(LAST, start, stop, piece_sem.at[i], None, [o])
     for i, (start, stop) in enumerate(PIECES):
-        ship(LAST, start, stop, piece_sem.at[i], self_sem.at[FULL + 1 + i])
+        ship(LAST, start, stop, piece_sem.at[i], self_sem.at[FULL + 1 + i], NEAR)
 
     for w in weight_loads:
         w.wait()
@@ -301,18 +308,14 @@
         rows = pl.ds(start, stop - start)
         last_surf[rows, :] = recv[LAST, 0, rows, :]
 
-    early = LEV - 3
+    early = EARLY_LEVELS
     piece(0)
     for j in range(2):
         gather(LAST, j)
-    for p in range(3):
-        embed(2 * p, 2)
-    for p in range(3):
-        attend(2 * p, 2)
-    piece(1)
-    gather(LAST, 2)
-    embed(6, 3)
-    attend(6, 3)
+    for p in range(0, early, 2):
+        embed(p, 2)
+    for p in range(0, early, 2):
+        attend(p, 2)
     top = scores[0]
     for l in range(1, early):
         top = jnp.maximum(top, scores[l])
@@ -325,15 +328,20 @@
     scores[0] = top
     scores[1] = total
 
-    piece(2)
-    gather(LAST, 3)
-    embed(early, 3)
-    attend(early, 3)
+    piece(1)
+    for j in range(2, FPD):
+        gather(LAST, j)
+    for p in range(early, LEV, 2):
+        embed(p, 2)
+    for p in range(early, LEV, 2):
+        attend(p, 2)
     last = [scores[l] for l in range(early, LEV)]
-    top = jnp.maximum(jnp.maximum(last[0], last[1]), jnp.maximum(last[2], scores[0]))
+    top = scores[0]
+    for x in last:
+        top = jnp.maximum(top, x)
     last = [jnp.exp(x - top) for x in last]
     scale = jnp.exp(scores[0] - top)
-    share = 1.0 / (last[0] + last[1] + last[2] + scale * scores[1])
+    share = 1.0 / (sum(last) + scale * scores[1])
     scores[0] = scale * share
     for i, e in enumerate(last):
         scores[early + i] = e * share

time: 112 us -> 111 us (level)
  no operation moved by 1% of the time
where the time goes in v4:
time: 111 us
  Pallas kernels  111 us (100%)
    pallas_call x1, Pallas kernels, shards(): pl.pallas_call(kernel, out_shape=[pltpu.VMEM((A, EARLY, LATENT + 1, C), B...  109 us

profile of v4, /device:TPU:1, one launch (start us, length us, event | category | flops | bytes accessed | tf_op | source)
XLA Modules:
  0.0 111.1 jit_solution(4130141740312381830)
XLA Ops:
  0.0 109.4 %exchange_and_encode.1 = (bf16[8,80,4,512]{3,2,1,0:T(4,128)(2,1)S(1)}, bf16[3,512,128]{2,1,0:T(8,128)(2,1)S(1)}, bf16[400,128]{1,0:T(8,128)(2,1)S(1)}, bf16[400,...) custom-call(bf16[90,400,128]{2,1,0:T(8,128)(2,1)} %bitcast.2, ...), custom_call_target="tpu_custom_call" | custom-call | tf_op jit(solution)/shard_map/exchange_and_encode/pallas_call | solution.py:390
  109.4 1.6 %finish.1 = bf16[8,90,4,512]{3,2,1,0:T(4,128)(2,1)} custom-call(bf16[8,80,4,512]{3,2,1,0:T(4,128)(2,1)S(1)} %get-tuple-element.11.staged, bf16[3,512,128]{2,1,0:T(8,128)(2,1)S(1)} %get-tuple-element.12.mix, bf16[400,128]{1,0:T(8,128)(2,1)S(1)} %get-tuple-element.13.last_surf, bf16[400,512]{1,0:T(8,128)(2,1)S(1)} %get-tuple-element.14.wsurf, ...), custom_call_target="tpu_custom_call" | custom-call | tf_op jit(solution)/shard_map/finish/pallas_call | solution.py:432

commit v5 on v4

--- a/solution.py
+++ b/solution.py
@@ -75,21 +75,21 @@
                 term = shares[i, pl.ds(m * HEADS + h, 1), :] * held[m]
                 sums[m] = term if sums[m] is None else sums[m] + term
         for m in range(LATENT):
-            out[m, rows, :] = sums[m].astype(out.dtype)
+            out[rows, pl.ds(m * LANES, LANES)] = sums[m].astype(out.dtype)
 
 
 def project(block, mix, wsurf, ow, lat, slots):
     contract = (((0,), (0,)), ((), ()))
     slots[:, 0, :] = lax.dot_general(block[...], wsurf[...], contract, preferred_element_type=F32)
+    agg = lax.dot_general(mix[...], ow[...], contract, preferred_element_type=F32)
     for m in range(LATENT):
-        agg = lax.dot_general(mix[m], ow[...], contract, preferred_element_type=F32)
-        slots[:, m + 1, :] = agg + lat[pl.ds(m, 1), :].astype(F32)
+        slots[:, m + 1, :] = agg[m * LANES : (m + 1) * LANES] + lat[pl.ds(m, 1), :].astype(F32)
 
 
 def kernel(
     fields_ref, surf_ref, atmos_ref, bias_ref, lat_ref, qm_ref, kw_ref, vw_ref, ow_ref,
-    staged, mix, last_surf, wsurf, ow_v, lat_v,
-    inb, send, recv, xs, wat, wuv, biasb, vals, scores, part, slots,
+    staged, vals, scores, part, last_surf, wsurf, ow_v, lat_v,
+    inb, send, recv, xs, wat, wuv, biasb, mix, slots,
     surf_v, atmos_v, bias_v, qm_v, kw_v, vw_v,
     in_sem, w_sem, send_sem, recv_sem, piece_sem, self_sem,
 ):
@@ -106,17 +106,6 @@
     for o in OFFSETS:
         pl.semaphore_signal(barrier, inc=1, device_id={"lat": peer_of(me, o)}, device_id_type=MESH)
     load(0, start=OPENING, sem=FULL + 1).start()
-    for c in range(1, FULL):
-        load(c).start()
-    load(FULL, REST).start()
-    weight_loads = []
-    for i, (src, dst) in enumerate((
-        (qm_ref, qm_v), (lat_ref, lat_v), (kw_ref, kw_v), (vw_ref, vw_v), (atmos_ref, atmos_v),
-        (surf_ref, surf_v), (bias_ref, bias_v), (ow_ref, ow_v),
-    )):
-        weight_loads.append(pltpu.make_async_copy(src, dst, w_sem.at[i]))
-        weight_loads[-1].start()
-
     def unturn(e, y):
         return y if e == 0 else pltpu.roll(y, LANES - 8 * e, 1)
 
@@ -170,9 +159,19 @@
     shuffle_full(0, stop=OPENING)
     pl.semaphore_wait(barrier, NDEV - 1)
     ship(0, 0, OPENING, recv_sem.at[0], self_sem.at[0])
+    for c in range(1, FULL):
+        load(c).start()
+    load(FULL, REST).start()
     load(0, start=OPENING, sem=FULL + 1).wait()
     shuffle_full(0, start=OPENING)
     ship(0, OPENING, ROWS, recv_sem.at[0], self_sem.at[0])
+    weight_loads = []
+    for i, (src, dst) in enumerate((
+        (qm_ref, qm_v), (lat_ref, lat_v), (kw_ref, kw_v), (vw_ref, vw_v), (atmos_ref, atmos_v),
+        (surf_ref, surf_v), (bias_ref, bias_v), (ow_ref, ow_v),
+    )):
+        weight_loads.append(pltpu.make_async_copy(src, dst, w_sem.at[i]))
+        weight_loads[-1].start()
 
     def send_next(c, carry):
         load(c).wait()
@@ -345,14 +344,13 @@
     scores[0] = scale * share
     for i, e in enumerate(last):
         scores[early + i] = e * share
-    mixture([(0, lambda m: part.at[m])] + [(l, vals.at[l]) for l in range(early, LEV)], scores, mix)
 
     for c in range(FULL + 1):
         whole = send.at[c, pl.ds(0, NDEV - 1), pl.ds(0, ROWS if c < FULL else REST_ROWS)]
         pltpu.make_async_copy(whole, whole, send_sem.at[c]).wait()
 
 
-def finish(staged, mix, last_surf, wsurf, ow, lat, out_ref, slots, outb, sem):
+def finish(staged, vals, scores, part, last_surf, wsurf, ow, lat, out_ref, mix, slots, outb, sem):
     ahead = BLK * LAST
     writes = [
         pltpu.make_async_copy(staged.at[:, pl.ds(0, ahead)], out_ref.at[:, pl.ds(0, ahead)], sem.at[0]),
@@ -360,6 +358,7 @@
     ]
     for write in writes:
         write.start()
+    mixture([(0, lambda m: part.at[:, pl.ds(m * LANES, LANES)])] + [(l, vals.at[l]) for l in range(EARLY_LEVELS, LEV)], scores, mix)
     project(last_surf, mix, wsurf, ow, lat, slots)
 
     def move(j, carry):
@@ -391,14 +390,16 @@
         kernel,
         out_shape=[
             pltpu.VMEM((A, EARLY, LATENT + 1, C), BF16),
-            pltpu.VMEM((LATENT, C, LANES), BF16),
+            pltpu.VMEM((LEV, C, LANES), F32),
+            pltpu.VMEM((LEV, QROWS, LANES), F32),
+            pltpu.VMEM((C, LATENT * LANES), F32),
             pltpu.VMEM((ROWS, LANES), BF16),
             pltpu.VMEM((NSURF * K, C), BF16),
             pltpu.VMEM((C, C), BF16),
             pltpu.VMEM((LATENT, C), BF16),
         ],
         in_specs=[in_hbm] * 9,
-        out_specs=[in_vmem] * 6,
+        out_specs=[in_vmem] * 8,
         scratch_shapes=[
             pltpu.VMEM((COLS, ROWS, LANES), BF16),
             pltpu.VMEM((FULL + 1, NDEV, ROWS, LANES), BF16),
@@ -407,9 +408,7 @@
             pltpu.VMEM((C, C), BF16),
             pltpu.VMEM((C + 2 * QROWS, C), BF16),
             pltpu.VMEM((LEV, C, LANES), F32),
-            pltpu.VMEM((LEV, C, LANES), F32),
-            pltpu.VMEM((LEV, QROWS, LANES), F32),
-            pltpu.VMEM((LATENT, C, LANES), F32),
+            pltpu.VMEM((C, LATENT * LANES), BF16),
             pltpu.VMEM((LANES, LATENT + 1, C), F32),
             pltpu.VMEM(surf_cells.shape, BF16),
             pltpu.VMEM(atmos_weight.shape, BF16),
@@ -432,9 +431,10 @@
     return pl.pallas_call(
         finish,
         out_shape=jax.ShapeDtypeStruct((A, COLS, LATENT + 1, C), BF16),
-        in_specs=[in_vmem] * 6,
+        in_specs=[in_vmem] * 8,
         out_specs=in_hbm,
         scratch_shapes=[
+            pltpu.VMEM((C, LATENT * LANES), BF16),
             pltpu.VMEM((LANES, LATENT + 1, C), F32),
             pltpu.VMEM((A, BLK, LATENT + 1, C), BF16),
             dma((4,)),

time: 111 us -> 111 us (level)
  no operation moved by 1% of the time
where the time goes in v5:
time: 111 us
  Pallas kernels  111 us (100%)
    pallas_call x1, Pallas kernels, shards(): pl.pallas_call(kernel, out_shape=[pltpu.VMEM((A, EARLY, LATENT + 1, C), B...  109 us

profile of v5, /device:TPU:1, one launch (start us, length us, event | category | flops | bytes accessed | tf_op | source)
XLA Modules:
  0.0 111.0 jit_solution(5233285425739312763)
XLA Ops:
  0.0 109.1 %exchange_and_encode.1 = (bf16[8,80,4,512]{3,2,1,0:T(4,128)(2,1)S(1)}, f32[12,512,128]{2,1,0:T(8,128)S(1)}, f32[12,48,128]{2,1,0:T(8,128)S(1)}, f32[512,384]{1,0...) custom-call(bf16[90,400,128]{2,1,0:T(8,128)(2,1)} %bitcast.2, ...), custom_call_target="tpu_custom_call" | custom-call | tf_op jit(solution)/shard_map/exchange_and_encode/pallas_call | solution.py:389
  109.1 1.8 %finish.1 = bf16[8,90,4,512]{3,2,1,0:T(4,128)(2,1)} custom-call(bf16[8,80,4,512]{3,2,1,0:T(4,128)(2,1)S(1)} %get-tuple-element.13.staged, f32[12,512,128]{2,1,0:T(8,128)S(1)} %get-tuple-element.14.vals, f32[12,48,128]{2,1,0:T(8,128)S(1)} %get-tuple-element.15.scores, f32[512,384]{1,0:T(8,128)S(1)} %get-tuple-element.16.part, ...), custom_call_target="tpu_custom_call" | custom-call | tf_op jit(solution)/shard_map/finish/pallas_call | solution.py:431

commit v6 on v5

--- a/solution.py
+++ b/solution.py
@@ -41,7 +41,12 @@
 
 def far_first():
     offsets = [(dy, dz, dc) for dy in range(4) for dz in range(2) for dc in range(2)][1:]
-    return sorted(offsets, key=lambda o: -(min(o[0], 4 - o[0]) + o[1]))
+
+    def rank(o):
+        far = min(o[0], 4 - o[0]) + o[1]
+        return -far, o[1] if far == 1 else 0
+
+    return sorted(offsets, key=rank)
 
 
 OFFSETS = far_first()
@@ -366,11 +371,12 @@
         for a in range(A):
             outb[a, j] = slots[start + a].astype(BF16)
         return carry
-    half = BLK // 2
-    for i in range(2):
-        lax.fori_loop(half * i, half * (i + 1), move, 0, unroll=4)
+    part_cols = BLK // 4
+    for i in range(4):
+        lax.fori_loop(part_cols * i, part_cols * (i + 1), move, 0, unroll=4)
         writes.append(pltpu.make_async_copy(
-            outb.at[:, pl.ds(half * i, half)], out_ref.at[:, pl.ds(ahead + half * i, half)], sem.at[2 + i]))
+            outb.at[:, pl.ds(part_cols * i, part_cols)],
+            out_ref.at[:, pl.ds(ahead + part_cols * i, part_cols)], sem.at[2 + i]))
         writes[-1].start()
     for write in writes:
         write.wait()
@@ -437,7 +443,7 @@
             pltpu.VMEM((C, LATENT * LANES), BF16),
             pltpu.VMEM((LANES, LATENT + 1, C), F32),
             pltpu.VMEM((A, BLK, LATENT + 1, C), BF16),
-            dma((4,)),
+            dma((6,)),
         ],
         compiler_params=pltpu.CompilerParams(vmem_limit_bytes=8 * 2**20),
         name="finish",

time: 111 us -> 111 us (level)
  no operation moved by 1% of the time
where the time goes in v6:
time: 111 us
  Pallas kernels  111 us (100%)
    pallas_call x1, Pallas kernels, shards(): pl.pallas_call(kernel, out_shape=[pltpu.VMEM((A, EARLY, LATENT + 1, C), B...  109 us

profile of v6, /device:TPU:1, one launch (start us, length us, event | category | flops | bytes accessed | tf_op | source)
XLA Modules:
  0.0 110.9 jit_solution(16252750607270410128)
XLA Ops:
  0.0 109.2 %exchange_and_encode.1 = (bf16[8,80,4,512]{3,2,1,0:T(4,128)(2,1)S(1)}, f32[12,512,128]{2,1,0:T(8,128)S(1)}, f32[12,48,128]{2,1,0:T(8,128)S(1)}, f32[512,384]{1,0...) custom-call(bf16[90,400,128]{2,1,0:T(8,128)(2,1)} %bitcast.2, ...), custom_call_target="tpu_custom_call" | custom-call | tf_op jit(solution)/shard_map/exchange_and_encode/pallas_call | solution.py:395
  109.2 1.8 %finish.1 = bf16[8,90,4,512]{3,2,1,0:T(4,128)(2,1)} custom-call(bf16[8,80,4,512]{3,2,1,0:T(4,128)(2,1)S(1)} %get-tuple-element.13.staged, f32[12,512,128]{2,1,0:T(8,128)S(1)} %get-tuple-element.14.vals, f32[12,48,128]{2,1,0:T(8,128)S(1)} %get-tuple-element.15.scores, f32[512,384]{1,0:T(8,128)S(1)} %get-tuple-element.16.part, ...), custom_call_target="tpu_custom_call" | custom-call | tf_op jit(solution)/shard_map/finish/pallas_call | solution.py:437

commit v7 on v5

--- a/solution.py
+++ b/solution.py
@@ -45,7 +45,7 @@
 
 
 OFFSETS = far_first()
-FAR = [o for o in OFFSETS if min(o[0], 4 - o[0]) + o[1] >= 2]
+FAR = [(0, 0, 1)] + [o for o in OFFSETS if min(o[0], 4 - o[0]) + o[1] >= 2]
 NEAR = [o for o in OFFSETS if o not in FAR]
 
 

time: 111 us -> 111 us (level)
  no operation moved by 1% of the time
where the time goes in v7:
time: 111 us
  Pallas kernels  111 us (100%)
    pallas_call x1, Pallas kernels, shards(): pl.pallas_call(kernel, out_shape=[pltpu.VMEM((A, EARLY, LATENT + 1, C), B...  109 us

profile of v7, /device:TPU:1, one launch (start us, length us, event | category | flops | bytes accessed | tf_op | source)
XLA Modules:
  0.0 111.0 jit_solution(14256408268215014848)
XLA Ops:
  0.0 109.1 %exchange_and_encode.1 = (bf16[8,80,4,512]{3,2,1,0:T(4,128)(2,1)S(1)}, f32[12,512,128]{2,1,0:T(8,128)S(1)}, f32[12,48,128]{2,1,0:T(8,128)S(1)}, f32[512,384]{1,0...) custom-call(bf16[90,400,128]{2,1,0:T(8,128)(2,1)} %bitcast.2, ...), custom_call_target="tpu_custom_call" | custom-call | tf_op jit(solution)/shard_map/exchange_and_encode/pallas_call | solution.py:389
  109.1 1.8 %finish.1 = bf16[8,90,4,512]{3,2,1,0:T(4,128)(2,1)} custom-call(bf16[8,80,4,512]{3,2,1,0:T(4,128)(2,1)S(1)} %get-tuple-element.13.staged, f32[12,512,128]{2,1,0:T(8,128)S(1)} %get-tuple-element.14.vals, f32[12,48,128]{2,1,0:T(8,128)S(1)} %get-tuple-element.15.scores, f32[512,384]{1,0:T(8,128)S(1)} %get-tuple-element.16.part, ...), custom_call_target="tpu_custom_call" | custom-call | tf_op jit(solution)/shard_map/finish/pallas_call | solution.py:431
